TPU v7x, 32 devices: a whole 2x2x4 slice. The times are simulated.
32 devices in a mesh: dp: 16 (over z, x, core), tensor: 2 (over y).
Axes of the slice: x: 2, y: 2, z: 4, core: 2. Of those that a mesh axis runs over, the one named last changes fastest.
Arguments:
- quant_rows: int32 [4096, 2048], P(('dp', 'tensor')), may hold values from -127 to 127
- residual: bfloat16 [4096, 2048], P(('dp', 'tensor')), may hold values from -48 to 48
- row_scale: float32 [4096], P(('dp', 'tensor')), may hold values from 0.004 to 0.04
- norm_gain: float32 [2048], replicated, may hold values from 0.1 to 1.9
- gate_pre: bfloat16 [4096, 7168], P('dp', 'tensor'), may hold values from -6 to 6
- up_pre: bfloat16 [4096, 7168], P('dp', 'tensor'), may hold values from -6 to 6
- hidden_grad: bfloat16 [4096, 7168], P('dp', 'tensor'), may hold values from -6 to 6
- gate_weight: bfloat16 [2048, 7168], P('dp', 'tensor'), may hold values from -0.125 to 0.125
- up_weight: bfloat16 [2048, 7168], P('dp', 'tensor'), may hold values from -0.125 to 0.125
Outputs:
- resid_grad: bfloat16 [4096, 2048], P(('dp', 'tensor'))
- gate_weight_grad: float32 [2048, 7168], P('dp', 'tensor')
- up_weight_grad: float32 [2048, 7168], P('dp', 'tensor')
All inputs are finite; a program needn't handle non-finite values.
Results may differ from a plain program's by a relative error of at most 0.014.
Values may be sent and summed in bfloat16 or wider, within the bound.
A program may use at most 128 MiB of HBM per device.

v0:
```python
import math

import jax
import jax.numpy as jnp
from jax import lax
from jax.sharding import PartitionSpec as P


def body(
    quant_rows,
    residual,
    row_scale,
    norm_gain,
    gate_pre,
    up_pre,
    hidden_grad,
    gate_weight,
    up_weight,
):
    summed_in = residual.astype(jnp.float32) + quant_rows.astype(jnp.float32) * row_scale[:, None]
    inverse = lax.rsqrt(jnp.mean(summed_in * summed_in, axis=-1, keepdims=True) + 1e-05)
    unit_rows = summed_in * inverse
    normed = (unit_rows * norm_gain).astype(jnp.bfloat16)
    gathered = lax.all_gather(normed, "tensor", axis=0, tiled=True)
    gate_val = gate_pre.astype(jnp.float32)
    up_val = up_pre.astype(jnp.float32)
    grad_val = hidden_grad.astype(jnp.float32)
    sigmoid_gate = jax.nn.sigmoid(gate_val)
    up_grad = (grad_val * gate_val * sigmoid_gate).astype(jnp.bfloat16)
    gate_grad = (grad_val * up_val * sigmoid_gate * (1.0 + gate_val * (1.0 - sigmoid_gate))).astype(
        jnp.bfloat16
    )
    grad_cat = jnp.concatenate((gate_grad, up_grad), axis=1)
    weight_cat = jnp.concatenate((gate_weight, up_weight), axis=1)
    partial_value = jnp.einsum(
        "rf,nf->rn",
        grad_cat,
        lax.all_gather(weight_cat, "dp", axis=0, tiled=True),
        preferred_element_type=jnp.float32,
    )
    normed_grad = lax.psum_scatter(
        partial_value.astype(jnp.bfloat16), "tensor", scatter_dimension=0, tiled=True
    ).astype(jnp.float32)
    grad_term = norm_gain * normed_grad
    input_grad = inverse * (
        grad_term - unit_rows * jnp.mean(unit_rows * grad_term, axis=-1, keepdims=True)
    )
    resid_grad = input_grad.astype(jnp.bfloat16)
    tokens_all = gate_pre.shape[0] * lax.axis_size("dp")
    factor = 1.0 / math.sqrt(tokens_all)
    weight_part = lax.dot_general(
        gathered, grad_cat, (((0,), (0,)), ((), ())), preferred_element_type=jnp.float32
    )
    own_rows = lax.psum_scatter(
        weight_part.astype(jnp.bfloat16), "dp", scatter_dimension=0, tiled=True
    ).astype(jnp.float32)
    scaled_grad = own_rows * factor
    hidden_width = gate_weight.shape[1]
    return (resid_grad, scaled_grad[:, :hidden_width], scaled_grad[:, hidden_width:])


def solution(mesh):
    placed = (
        P(("dp", "tensor"), None),
        P(("dp", "tensor"), None),
        P(("dp", "tensor")),
        P(),
        P("dp", "tensor"),
        P("dp", "tensor"),
        P("dp", "tensor"),
        P("dp", "tensor"),
        P("dp", "tensor"),
    )
    return jax.shard_map(
        body,
        mesh=mesh,
        in_specs=placed,
        out_specs=(P(("dp", "tensor"), None), P("dp", "tensor"), P("dp", "tensor")),
        check_vma=False,
    )
```

profile of v0, /device:TPU:0, one launch (start us, length us, event | category | flops | bytes accessed | tf_op | source)
XLA Modules:
  0.0 525.4 jit_solution(18109282726652698077)
XLA Ops:
  7.2 0.0 all-gather.3.cloned.1.call-start
  7.2 2.8 pad_maximum_fusion.3
  10.1 0.0 all-gather.3.cloned.1.call-update
  10.1 0.0 reduce-scatter.3.cloned.1.call-start
  10.1 4.6 fusion.2
  14.7 146.6 %all-gather.3.cloned.1.call-done = bf16[2048,7168]{1,0:T(8,128)(2,1)} async-done(((bf16[128,7168]{1,0:T(8,128)(2,1)}), bf16[2048,7168]{1,0:T(8,128)(2,1)}) %all-gather.3.cloned.1.call-update) | async-done | bytes 29360144 | tf_op jit(solution)/shard_map/all_gather | solution.py:38
  161.3 0.0 copy-start
  161.3 0.0 copy-start.1
  161.3 0.0 copy-start.3
  161.3 0.0 copy-start.2
  161.3 14.9 %convolution_convert_fusion.1 = bf16[256,2048]{1,0:T(8,128)(2,1)} fusion(bf16[2048,7168]{1,0:T(8,128)(2,1)} %all-gather.3.cloned.1.call-done, bf16[256,3584]{1,0:T(8,128)(2,1)} %get-tuple-element.6, bf16[256,3584]{1,0:T(8,128)(2,1)S(1)} %get-tuple-element.5), kind=kOutput, calls=%fused_computation.16 | convolution fusion | flops 7524057088 | bytes 34078720 | tf_op jit(solution)/shard_map/rf,nf->rn/dot_general | solution.py:35
  176.2 0.0 reduce-scatter.3.cloned.1.call-update
  176.2 0.0 all-gather.5.cloned.1.call-start
  176.3 0.0 copy-done
  176.3 0.0 copy-done.1
  176.3 0.0 copy-done.3
  176.3 0.4 multiply_reduce_fusion.1
  176.7 20.0 %reduce-scatter.3.cloned.1.call-done = bf16[128,2048]{1,0:T(8,128)(2,1)} async-done(((bf16[256,2048]{1,0:T(8,128)(2,1)}), bf16[128,2048]{1,0:T(8,128)(2,1)}) %reduce-scatter.3.cloned.1.call-update) | async-done | bytes 524304 | tf_op jit(solution)/shard_map/reduce_scatter | solution.py:41
  196.7 0.0 copy-done.2
  196.7 1.5 multiply_reduce_fusion
  198.2 2.5 multiply_convert_fusion
  200.7 0.0 all-gather.5.cloned.1.call-update
  200.8 0.0 reduce-scatter.5.cloned.1.call-start
  200.8 21.4 %all-gather.5.cloned.1.call-done = bf16[256,2048]{1,0:T(8,128)(2,1)} async-done(((bf16[128,2048]{1,0:T(8,128)(2,1)}), bf16[256,2048]{1,0:T(8,128)(2,1)}) %all-gather.5.cloned.1.call-update) | async-done | bytes 1048592 | tf_op jit(solution)/shard_map/all_gather | solution.py:24
  222.2 14.7 %convolution_convert_fusion = bf16[2048,7168]{1,0:T(8,128)(2,1)} fusion(bf16[256,2048]{1,0:T(8,128)(2,1)} %all-gather.5.cloned.1.call-done, bf16[256,3584]{1,0:T(8,128)(2,1)} %get-tuple-element.6, bf16[256,3584]{1,0:T(8,128)(2,1)S(1)} %get-tuple-element.5), kind=kOutput, calls=%fused_computation | convolution fusion | flops 7538212864 | bytes 34078720 | tf_op jit(solution)/shard_map/dot_general | solution.py:51
  237.0 0.0 reduce-scatter.5.cloned.1.call-update
  237.0 277.9 %reduce-scatter.5.cloned.1.call-done = bf16[128,7168]{1,0:T(8,128)(2,1)} async-done(((bf16[2048,7168]{1,0:T(8,128)(2,1)}), bf16[128,7168]{1,0:T(8,128)(2,1)}) %reduce-scatter.5.cloned.1.call-update) | async-done | bytes 1835024 | tf_op jit(solution)/shard_map/reduce_scatter | solution.py:54
  514.9 1.9 convert_multiply_fusion.3
  516.8 2.1 fusion.11
  (2 shorter events, 0.0 us)
Async XLA Ops:
  7.2 154.1 %all-gather.3.cloned.1.call-start = ((), (), s32[]{:S(2)}) async-start(), calls=%async_computation.2 | async-start | bytes 31195136 | tf_op jit(solution)/shard_map/all_gather | solution.py:38
  10.1 186.6 %reduce-scatter.3.cloned.1.call-start = ((), (), s32[]{:S(2)}) async-start(), calls=%async_computation.3 | async-start | bytes 1572864 | tf_op jit(solution)/shard_map/reduce_scatter | solution.py:41
  161.3 15.0 %copy-start = (s32[128,2048]{1,0:T(8,128)S(1)}, s32[128,2048]{1,0:T(8,128)}, u32[]{:S(2)}) copy-start(s32[128,2048]{1,0:T(8,128)} %param.9) | copy-start | bytes 3145732
  161.3 15.0 %copy-start.1 = (bf16[128,2048]{1,0:T(8,128)(2,1)S(1)}, bf16[128,2048]{1,0:T(8,128)(2,1)}, u32[]{:S(2)}) copy-start(bf16[128,2048]{1,0:T(8,128)(2,1)} %param.10) | copy-start | bytes 1572868
  161.3 15.0 %copy-start.3 = (f32[128]{0:T(128)S(1)}, f32[128]{0:T(128)}, u32[]{:S(2)}) copy-start(f32[128]{0:T(128)} %param.11) | copy-start | bytes 1540
  161.3 35.4 %copy-start.2 = (f32[2048]{0:T(1024)S(1)}, f32[2048]{0:T(1024)}, u32[]{:S(2)}) copy-start(f32[2048]{0:T(1024)} %param.12) | copy-start | bytes 24580
  176.2 46.0 %all-gather.5.cloned.1.call-start = ((), (), s32[]{:S(2)}) async-start(), calls=%async_computation.4 | async-start | bytes 1572864 | tf_op jit(solution)/shard_map/all_gather | solution.py:24
  200.8 314.1 %reduce-scatter.5.cloned.1.call-start = ((), (), s32[]{:S(2)}) async-start(), calls=%async_computation.5 | async-start | bytes 31195136 | tf_op jit(solution)/shard_map/reduce_scatter | solution.py:54
Sparse Core Ops, SparseCore 0:
  10.2 151.0 all-gather.2
  176.4 20.3 reduce-scatter.2
  200.9 21.2 all-gather.4
  237.1 277.7 reduce-scatter.4
where the time goes:
time: 526 us; the launch traced here: 525 us
  waiting for transfers between devices  466 us (89%)
  matrix products  29.7 us (6%)
  between operations  13.8 us (3%)
  other arithmetic  13.7 us (3%)
    reduce_scatter x1, waiting for transfers between devices, body(): lax.psum_scatter(weight_part.astype(jnp.bfloat16), 'dp', scatter_dimensio...  278 us
    all_gather x1, waiting for transfers between devices, body(): lax.all_gather(weight_cat, 'dp', axis=0, tiled=True)  147 us
    all_gather x1, waiting for transfers between devices, body(): gathered = lax.all_gather(normed, 'tensor', axis=0, tiled=True)  21.4 us
    reduce_scatter x1, waiting for transfers between devices, body(): lax.psum_scatter(partial_value.astype(jnp.bfloat16), 'tensor', scatter_di...  20 us
    dot_general x1, matrix products, body(): jnp.einsum('rf,nf->rn', grad_cat, lax.all_gather(weight_cat, 'dp', axis=0...  14.9 us
    dot_general x1, matrix products, body(): lax.dot_general(gathered, grad_cat, (((0,), (0,)), ((), ())), preferred_e...  14.7 us
  transfers between devices with their start and end apart: 4, of which 4 were waited for; matrix products, arithmetic and copies ran while one was open for 1% of the time, Pallas kernels for 0%

commit v1 on v0

v1 whole, which is shorter than its diff:
```python
import functools
import math

import jax
import jax.numpy as jnp
from jax import lax
from jax.experimental import pallas as pl
from jax.experimental.pallas import tpu as pltpu
from jax.sharding import PartitionSpec as P

MESH = pl.DeviceIdType.MESH
BF16 = jnp.bfloat16
F32 = jnp.float32
CORES = 2


def line_length(dp):
    for length in (4, 2):
        if dp % (length * CORES) == 0:
            return length
    return 1


def chunk_count(width):
    for count in (7, 4, 2):
        if width % (count * 128) == 0:
            return count
    return 1


def fused_kernel(
    dims,
    factor,
    normed_ref,
    gate_ref,
    up_ref,
    hidden_ref,
    gate_w_ref,
    up_w_ref,
    grad_out,
    gate_out,
    up_out,
    acts,
    weights,
    rs_send,
    rs_recv,
    normed_all,
    acc,
    ng_send,
    ng_recv,
    ag_ss,
    ag_rs,
    rs_ss,
    rs_rs,
    gx_ss,
    gx_rs,
    gc_ss,
    gc_rs,
    n_ss,
    n_rs,
    ng_ss,
    ng_rs,
):
    Z, I, NT, NC, CW = dims
    X = I // CORES
    S = I * NT
    slab = gate_ref.shape[0]
    rows = gate_w_ref.shape[0]
    tok = slab // NT
    dp = lax.axis_index("dp")
    y = lax.axis_index("tensor")
    z = lax.div(dp, I)
    i = lax.rem(dp, I)
    x = lax.div(i, CORES)
    c = lax.rem(i, CORES)
    me = i * NT + y
    base = z * I
    partner = (base + x * CORES + (1 - c), y)
    right = (dp + I, y)
    left = (dp - I, y)

    def member(s):
        return (base + lax.div(s, NT), lax.rem(s, NT))

    def across(other):
        return (base + other * CORES + c, y)

    def copy(src, dst, send_sem, recv_sem, device):
        return pltpu.make_async_remote_copy(
            src_ref=src, dst_ref=dst, send_sem=send_sem, recv_sem=recv_sem,
            device_id=device, device_id_type=MESH,
        )

    barrier = pltpu.get_barrier_semaphore()

    @pl.loop(0, S)
    def _(s):
        @pl.when(s != me)
        def _():
            pl.semaphore_signal(barrier, inc=1, device_id=member(s), device_id_type=MESH)

    @pl.when(z < Z - 1)
    def _():
        pl.semaphore_signal(barrier, inc=1, device_id=right, device_id_type=MESH)

    @pl.when(z > 0)
    def _():
        pl.semaphore_signal(barrier, inc=1, device_id=left, device_id_type=MESH)

    @pl.loop(0, NC)
    def _(k):
        columns = pl.ds(pl.multiple_of(k * CW, 128), CW)
        weights[k, 0, z] = gate_w_ref[:, columns]
        weights[k, 1, z] = up_w_ref[:, columns]

    inside = (z > 0) & (z < Z - 1)

    @pl.when(inside)
    def _():
        pl.semaphore_wait(barrier, S + 1)

    @pl.when(jnp.logical_not(inside))
    def _():
        pl.semaphore_wait(barrier, S if Z > 1 else S - 1)

    def ag_right(k, origin):
        block = weights.at[k, :, origin]
        return copy(block, block, ag_ss.at[k, 0, origin], ag_rs.at[k, origin], right)

    def ag_left(k, origin):
        block = weights.at[k, :, origin]
        return copy(block, block, ag_ss.at[k, 1, origin], ag_rs.at[k, origin], left)

    def normed_copy(s, source):
        place = pl.ds(pl.multiple_of(source * tok, 128), tok)
        return copy(
            normed_ref.at[lax.div(s, NT)], normed_all.at[:, place], n_ss.at[s], n_rs.at[source], member(s)
        )

    @pl.loop(0, S)
    def _(s):
        @pl.when(s != me)
        def _():
            normed_copy(s, me).start()

    @pl.loop(0, NC)
    def _(k):
        @pl.when(z < Z - 1)
        def _():
            ag_right(k, z).start()

        @pl.when(z > 0)
        def _():
            ag_left(k, z).start()

    normed_all[:, pl.ds(pl.multiple_of(me * tok, 128), tok)] = normed_ref[i]

    def act_across(k, other, source):
        block = acts.at[k, :, source * CORES + c]
        return copy(block, block, gx_ss.at[k, other], gx_rs.at[k, source], across(other))

    def act_partner(k, source_x, source_c):
        block = acts.at[k, :, source_x * CORES + source_c]
        return copy(block, block, gc_ss.at[k, source_x], gc_rs.at[k, source_x], partner)

    part = 32

    @pl.loop(0, NC)
    def _(k):
        columns = pl.ds(pl.multiple_of(k * CW, 128), CW)

        @pl.loop(0, slab // part)
        def _(r):
            span = pl.ds(pl.multiple_of(r * part, part), part)
            gate_val = gate_ref[span, columns].astype(F32)
            up_val = up_ref[span, columns].astype(F32)
            grad_val = hidden_ref[span, columns].astype(F32)
            sig = 1.0 / (1.0 + jnp.exp(-gate_val))
            scaled = grad_val * sig
            acts[k, 1, i, span] = (scaled * gate_val).astype(BF16)
            acts[k, 0, i, span] = (scaled * up_val * (1.0 + gate_val * (1.0 - sig))).astype(BF16)

        @pl.loop(0, X)
        def _(other):
            @pl.when(other != x)
            def _():
                act_across(k, other, x).start()

        act_partner(k, x, c).start()

    def rs_right(k, d):
        return copy(rs_send.at[k, d], rs_recv.at[k, d], rs_ss.at[k, d], rs_rs.at[k, d], right)

    def rs_left(k, d, slot):
        return copy(rs_send.at[k, d], rs_recv.at[k, slot], rs_ss.at[k, d], rs_rs.at[k, slot], left)

    def add_in(k, d):
        for t in range(2):
            rs_send[k, d, t] = (rs_send[k, d, t].astype(F32) + rs_recv[k, d, t].astype(F32)).astype(BF16)

    @pl.loop(0, S)
    def _(s):
        @pl.when(s != me)
        def _():
            normed_copy(s, s).wait_recv()

    @pl.loop(0, NC + max(Z - 2, 0))
    def _(it):
        @pl.when(it < NC)
        def _():
            @pl.loop(0, X)
            def _(other):
                @pl.when(other != x)
                def _():
                    act_across(it, other, other).wait_recv()
                    act_partner(it, other, c).start()

            @pl.loop(0, X)
            def _(other):
                act_partner(it, other, 1 - c).wait_recv()

            for t in range(2):
                full = jnp.zeros((Z * rows, CW), F32)
                for j in range(I):
                    full = full + jnp.dot(
                        normed_all[:, j * slab : (j + 1) * slab], acts[it, t, j],
                        preferred_element_type=F32,
                    )
                for d in range(Z):
                    rs_send[it, d, t] = full[d * rows : (d + 1) * rows].astype(BF16)

        kr = it - z

        @pl.when((kr >= 0) & (kr < NC) & (z < Z - 1))
        def _():
            for d in range(Z - 1, 0, -1):
                @pl.when(d > z)
                def _():
                    @pl.when(z > 0)
                    def _():
                        rs_right(kr, d).wait_recv()
                        add_in(kr, d)

                    rs_right(kr, d).start()

        kl = it - (Z - 1 - z)

        @pl.when((kl >= 0) & (kl < NC) & (z > 0))
        def _():
            for d in range(Z - 1):
                @pl.when(d < z)
                def _():
                    @pl.when(z < Z - 1)
                    def _():
                        rs_left(kl, d, d).wait_recv()
                        add_in(kl, d)

                    @pl.when(d < z - 1)
                    def _():
                        rs_left(kl, d, d).start()

                    @pl.when(d == z - 1)
                    def _():
                        rs_left(kl, d, Z).start()

        for h in range(1, Z - 1):
            kh = it - h

            @pl.when((kh >= 0) & (kh < NC) & (z >= h) & (z < Z - 1))
            def _():
                ag_right(kh, z - h).wait_recv()
                ag_right(kh, z - h).start()

            @pl.when((kh >= 0) & (kh < NC) & (z + h < Z) & (z > 0))
            def _():
                ag_left(kh, z + h).wait_recv()
                ag_left(kh, z + h).start()

    @pl.loop(0, NC)
    def _(k):
        for o in range(Z):
            @pl.when((z == Z - 1) & (z != o))
            def _():
                ag_left(k, o).wait_recv()

            @pl.when((z == 0) & (z != o))
            def _():
                ag_right(k, o).wait_recv()

    def ng_copy(s, source):
        return copy(ng_send.at[s], ng_recv.at[source], ng_ss.at[s], ng_rs.at[source], member(s))

    @pl.loop(0, I)
    def _(j):
        acc[...] = jnp.zeros_like(acc)

        @pl.loop(0, NC)
        def _(k):
            for t in range(2):
                acc[...] += lax.dot_general(
                    acts[k, t, j], weights[k, t].reshape(Z * rows, CW),
                    (((1,), (1,)), ((), ())), preferred_element_type=F32,
                )

        @pl.loop(0, NT)
        def _(h):
            s = j * NT + h
            ng_send[s] = acc[pl.ds(pl.multiple_of(h * tok, 128), tok), :].astype(BF16)

            @pl.when(s != me)
            def _():
                ng_copy(s, me).start()

    ng_recv[me] = ng_send[me]

    @pl.loop(0, NC)
    def _(k):
        columns = pl.ds(pl.multiple_of(k * CW, 128), CW)
        gate_out[:, columns] = rs_send[k, z, 0].astype(F32) * factor
        up_out[:, columns] = rs_send[k, z, 1].astype(F32) * factor

        @pl.when(z > 0)
        def _():
            rs_right(k, z).wait_recv()
            gate_out[:, columns] += rs_recv[k, z, 0].astype(F32) * factor
            up_out[:, columns] += rs_recv[k, z, 1].astype(F32) * factor

        @pl.when(z < Z - 1)
        def _():
            rs_left(k, z, Z).wait_recv()
            gate_out[:, columns] += rs_recv[k, Z, 0].astype(F32) * factor
            up_out[:, columns] += rs_recv[k, Z, 1].astype(F32) * factor

    @pl.loop(0, S)
    def _(s):
        @pl.when(s != me)
        def _():
            ng_copy(s, s).wait_recv()

    @pl.loop(0, I)
    def _(j):
        total = ng_recv[j * NT].astype(F32)
        for h in range(1, NT):
            total = total + ng_recv[j * NT + h].astype(F32)
        grad_out[j] = total

    @pl.loop(0, S)
    def _(s):
        @pl.when(s != me)
        def _():
            normed_copy(s, me).wait_send()
            ng_copy(s, me).wait_send()

    @pl.loop(0, NC)
    def _(k):
        @pl.loop(0, X)
        def _(other):
            act_partner(k, other, c).wait_send()

            @pl.when(other != x)
            def _():
                act_across(k, other, x).wait_send()

        for d in range(Z):
            @pl.when(d > z)
            def _():
                rs_right(k, d).wait_send()

            @pl.when(d < z)
            def _():
                rs_left(k, d, d).wait_send()

            @pl.when((z < Z - 1) & (d <= z))
            def _():
                ag_right(k, d).wait_send()

            @pl.when((z > 0) & (d >= z))
            def _():
                ag_left(k, d).wait_send()


def fused(dims, factor, normed, gate_pre, up_pre, hidden_grad, gate_weight, up_weight):
    Z, I, NT, NC, CW = dims
    X = I // CORES
    S = I * NT
    slab = gate_pre.shape[0]
    rows, width = gate_weight.shape
    tok = slab // NT
    depth = Z * rows
    dma = pltpu.SemaphoreType.DMA
    vmem = pl.BlockSpec(memory_space=pltpu.VMEM)
    return pl.pallas_call(
        functools.partial(fused_kernel, dims, factor),
        out_shape=(
            jax.ShapeDtypeStruct((I, tok, depth), F32),
            jax.ShapeDtypeStruct((rows, width), F32),
            jax.ShapeDtypeStruct((rows, width), F32),
        ),
        in_specs=[vmem] * 6,
        out_specs=(vmem, vmem, vmem),
        scratch_shapes=[
            pltpu.VMEM((NC, 2, I, slab, CW), BF16),
            pltpu.VMEM((NC, 2, Z, rows, CW), BF16),
            pltpu.VMEM((NC, Z, 2, rows, CW), BF16),
            pltpu.VMEM((NC, Z + 1, 2, rows, CW), BF16),
            pltpu.VMEM((depth, S * tok), BF16),
            pltpu.VMEM((slab, depth), F32),
            pltpu.VMEM((S, tok, depth), BF16),
            pltpu.VMEM((S, tok, depth), BF16),
            dma((NC, 2, Z)),
            dma((NC, Z)),
            dma((NC, Z)),
            dma((NC, Z + 1)),
            dma((NC, X)),
            dma((NC, X)),
            dma((NC, X)),
            dma((NC, X)),
            dma((S,)),
            dma((S,)),
            dma((S,)),
            dma((S,)),
        ],
        compiler_params=pltpu.CompilerParams(
            collective_id=0, has_side_effects=True, vmem_limit_bytes=61 * 1024 * 1024
        ),
        cost_estimate=pl.CostEstimate(
            flops=8 * slab * I * depth * width, bytes_accessed=20 * 1024 * 1024, transcendentals=slab * width
        ),
    )(normed, gate_pre, up_pre, hidden_grad, gate_weight, up_weight)


def body(
    quant_rows,
    residual,
    row_scale,
    norm_gain,
    gate_pre,
    up_pre,
    hidden_grad,
    gate_weight,
    up_weight,
):
    count = lax.axis_size("dp")
    tensor = lax.axis_size("tensor")
    Z = line_length(count)
    I = count // Z
    tok, depth = residual.shape
    rows = gate_weight.shape[0]
    NC = chunk_count(gate_weight.shape[1])
    CW = gate_weight.shape[1] // NC
    summed_in = residual.astype(F32) + quant_rows.astype(F32) * row_scale[:, None]
    inverse = lax.rsqrt(jnp.mean(summed_in * summed_in, axis=-1, keepdims=True) + 1e-05)
    unit_rows = summed_in * inverse
    normed = (unit_rows * norm_gain).astype(BF16)
    blocks = normed.reshape(tok, Z, I, rows).transpose(2, 1, 3, 0).reshape(I, Z * rows, tok)
    factor = 1.0 / math.sqrt(gate_pre.shape[0] * count)
    summed, gate_out, up_out = fused(
        (Z, I, tensor, NC, CW), factor, blocks, gate_pre, up_pre, hidden_grad, gate_weight, up_weight
    )
    normed_grad = summed.reshape(I, tok, Z, rows).transpose(1, 2, 0, 3).reshape(tok, depth)
    grad_term = norm_gain * normed_grad
    input_grad = inverse * (
        grad_term - unit_rows * jnp.mean(unit_rows * grad_term, axis=-1, keepdims=True)
    )
    return (input_grad.astype(BF16), gate_out, up_out)


def solution(mesh):
    placed = (
        P(("dp", "tensor"), None),
        P(("dp", "tensor"), None),
        P(("dp", "tensor")),
        P(),
        P("dp", "tensor"),
        P("dp", "tensor"),
        P("dp", "tensor"),
        P("dp", "tensor"),
        P("dp", "tensor"),
    )
    return jax.shard_map(
        body,
        mesh=mesh,
        in_specs=placed,
        out_specs=(P(("dp", "tensor"), None), P("dp", "tensor"), P("dp", "tensor")),
        check_vma=False,
    )
```

time: 526 us -> 231 us (0.44)
  waiting for transfers between devices: 466 us -> 0 us
  Pallas kernels: 0 us -> 215 us
  matrix products: 29.7 us -> 0 us
  between operations: 13.8 us -> 0.72 us
  other arithmetic: 13.7 us -> 4.67 us
  local copies, waits for them, and re-layouts: 2.12 us -> 10.2 us
    reduce_scatter x2 -> x0, waiting for transfers between devices: 298 us -> none  [the longest x1 278 us: body(): lax.psum_scatter(weight_part.astype(jnp.bfloat16), 'dp', scatter_dimensio...]
    pallas_call x0 -> x1, Pallas kernels: none -> 215 us  [fused(): pl.pallas_call(functools.partial(fused_kernel, dims, factor), out_shape=(...]
    all_gather x2 -> x0, waiting for transfers between devices: 168 us -> none  [the longest x1 147 us: body(): lax.all_gather(weight_cat, 'dp', axis=0, tiled=True)]
    dot_general x2 -> x0, matrix products: 29.7 us -> none  [the longest x1 14.9 us: body(): jnp.einsum('rf,nf->rn', grad_cat, lax.all_gather(weight_cat, 'dp', axis=0...]
  transfers between devices with their start and end apart: 4 -> 0, of which waited for: 4 -> 0; matrix products, arithmetic and copies ran while one was open for 1% -> 0% of each run, Pallas kernels for 0% -> 0%
where the time goes in v1:
time: 231 us
  Pallas kernels  215 us (93%)
  local copies, waits for them, and re-layouts  10.2 us (4%)
  other arithmetic  4.67 us (2%)
    pallas_call x1, Pallas kernels, fused(): pl.pallas_call(functools.partial(fused_kernel, dims, factor), out_shape=(...  215 us

profile of v1, /device:TPU:0, one launch (start us, length us, event | category | flops | bytes accessed | tf_op | source)
XLA Modules:
  0.0 230.9 jit_solution(6809953169645517048)
XLA Ops:
  0.6 0.0 copy-start.1
  0.6 0.0 copy-start
  0.7 1.8 multiply_reduce_fusion.1
  2.5 0.0 copy-done.1
  2.5 0.0 copy-done
  2.5 1.1 multiply_convert_fusion.1
  3.6 0.4 reshape.32
  4.0 1.2 copy.12
  5.2 215.3 %shard_map.112 = (f32[4,128,512]{2,1,0:T(8,128)}, f32[128,3584]{1,0:T(8,128)}, f32[128,3584]{1,0:T(8,128)}) custom-call(bf16[4,512,128]{2,1,0:T(8,128)(2,1)} %bitcast.5, bf16[256,3584]{1,0:T(8,128)(2,1)} %gate_ref.1, bf16[256,3584]{1,0:T(8,128)(2,1)} %up_ref.1, bf16[256,3584]{1,0:T(8,128)(2,1)} %hidden_ref.1, bf16[128,3584]{1,0:T(8,128)(2,1)} %gate_w_ref.1, ...), custom_call_target="tpu_custom_call" | custom-call | flops 15032385536 | bytes 20971520 | tf_op jit(solution)/shard_map/pallas_call | solution.py:392
  220.5 1.6 reshape.34
  222.1 0.0 copy-start.4
  222.1 0.0 copy-start.5
  222.1 1.6 copy.13
  223.8 1.6 reshape.35
  225.4 0.0 copy-done.4
  225.4 0.0 copy-done.5
  225.4 0.4 multiply_reduce_fusion
  225.9 0.0 copy-start.3
  225.9 1.3 multiply_convert_fusion
  227.2 0.3 copy-done.3
  227.5 0.0 copy-start.2
  227.5 1.2 copy.16
  228.7 0.9 copy-done.2
  229.7 1.2 copy.17
  (2 shorter events, 0.0 us)
Async XLA Ops:
  0.6 1.9 copy-start.1
  0.6 1.9 copy-start
  222.1 3.3 %copy-start.4 = (f32[2048]{0:T(1024)S(1)}, f32[2048]{0:T(1024)}, u32[]{:S(2)}) copy-start(f32[2048]{0:T(1024)} %param.12) | copy-start | bytes 24580
  222.1 3.3 %copy-start.5 = (f32[128]{0:T(128)S(1)}, f32[128]{0:T(128)}, u32[]{:S(2)}) copy-start(f32[128]{0:T(128)} %param.11) | copy-start | bytes 1540
  225.9 1.6 copy-start.3
  227.5 2.2 copy-start.2

commit v2 on v1

--- a/solution.py
+++ b/solution.py
@@ -37,6 +37,9 @@
     hidden_ref,
     gate_w_ref,
     up_w_ref,
+    unit_ref,
+    inverse_ref,
+    gain_ref,
     grad_out,
     gate_out,
     up_out,
@@ -48,6 +51,7 @@
     acc,
     ng_send,
     ng_recv,
+    terms,
     ag_ss,
     ag_rs,
     rs_ss,
@@ -206,6 +210,19 @@
 
     @pl.loop(0, NC + max(Z - 2, 0))
     def _(it):
+        for h in range(1, Z - 1):
+            kh = it - h
+
+            @pl.when((kh >= 0) & (kh < NC) & (z >= h) & (z < Z - 1))
+            def _():
+                ag_right(kh, z - h).wait_recv()
+                ag_right(kh, z - h).start()
+
+            @pl.when((kh >= 0) & (kh < NC) & (z + h < Z) & (z > 0))
+            def _():
+                ag_left(kh, z + h).wait_recv()
+                ag_left(kh, z + h).start()
+
         @pl.when(it < NC)
         def _():
             @pl.loop(0, X)
@@ -229,69 +246,32 @@
                 for d in range(Z):
                     rs_send[it, d, t] = full[d * rows : (d + 1) * rows].astype(BF16)
 
-        kr = it - z
-
-        @pl.when((kr >= 0) & (kr < NC) & (z < Z - 1))
-        def _():
-            for d in range(Z - 1, 0, -1):
-                @pl.when(d > z)
-                def _():
-                    @pl.when(z > 0)
-                    def _():
-                        rs_right(kr, d).wait_recv()
-                        add_in(kr, d)
-
-                    rs_right(kr, d).start()
-
-        kl = it - (Z - 1 - z)
-
-        @pl.when((kl >= 0) & (kl < NC) & (z > 0))
-        def _():
-            for d in range(Z - 1):
-                @pl.when(d < z)
-                def _():
-                    @pl.when(z < Z - 1)
-                    def _():
-                        rs_left(kl, d, d).wait_recv()
-                        add_in(kl, d)
-
-                    @pl.when(d < z - 1)
-                    def _():
-                        rs_left(kl, d, d).start()
-
-                    @pl.when(d == z - 1)
-                    def _():
-                        rs_left(kl, d, Z).start()
-
-        for h in range(1, Z - 1):
-            kh = it - h
-
-            @pl.when((kh >= 0) & (kh < NC) & (z >= h) & (z < Z - 1))
-            def _():
-                ag_right(kh, z - h).wait_recv()
-                ag_right(kh, z - h).start()
-
-            @pl.when((kh >= 0) & (kh < NC) & (z + h < Z) & (z > 0))
-            def _():
-                ag_left(kh, z + h).wait_recv()
-                ag_left(kh, z + h).start()
-
-    @pl.loop(0, NC)
-    def _(k):
-        for o in range(Z):
-            @pl.when((z == Z - 1) & (z != o))
-            def _():
-                ag_left(k, o).wait_recv()
-
-            @pl.when((z == 0) & (z != o))
-            def _():
-                ag_right(k, o).wait_recv()
+            @pl.when((z == 0) & (Z > 1))
+            def _():
+                for d in range(Z - 1, 0, -1):
+                    rs_right(it, d).start()
+
+            @pl.when((z == Z - 1) & (Z > 1))
+            def _():
+                for d in range(Z - 1):
+                    rs_left(it, d, d if d < Z - 2 else Z).start()
 
     def ng_copy(s, source):
         return copy(ng_send.at[s], ng_recv.at[source], ng_ss.at[s], ng_rs.at[source], member(s))
 
-    @pl.loop(0, I)
-    def _(j):
+    def weights_there():
+        @pl.loop(0, NC)
+        def _(k):
+            for o in range(Z):
+                @pl.when((z == Z - 1) & (z != o))
+                def _():
+                    ag_left(k, o).wait_recv()
+
+                @pl.when((z == 0) & (z != o))
+                def _():
+                    ag_right(k, o).wait_recv()
+
+    def normed_gradient(j):
         acc[...] = jnp.zeros_like(acc)
 
         @pl.loop(0, NC)
@@ -311,7 +291,63 @@
             def _():
                 ng_copy(s, me).start()
 
+    weights_there()
+
+    @pl.loop(0, max(NC + max(Z - 3, 0), I + 1))
+    def _(it):
+        kr = it - jnp.maximum(z - 1, 0)
+
+        @pl.when((kr >= 0) & (kr < NC) & (z > 0) & (z < Z - 1))
+        def _():
+            for d in range(Z - 1, 1, -1):
+                @pl.when(d > z)
+                def _():
+                    rs_right(kr, d).wait_recv()
+                    add_in(kr, d)
+                    rs_right(kr, d).start()
+
+        kl = it - jnp.maximum(Z - 2 - z, 0)
+
+        @pl.when((kl >= 0) & (kl < NC) & (z > 0) & (z < Z - 1))
+        def _():
+            for d in range(Z - 2):
+                @pl.when(d < z)
+                def _():
+                    rs_left(kl, d, d).wait_recv()
+                    add_in(kl, d)
+
+                    @pl.when(d < z - 1)
+                    def _():
+                        rs_left(kl, d, d).start()
+
+                    @pl.when(d == z - 1)
+                    def _():
+                        rs_left(kl, d, Z).start()
+
+        @pl.when((it >= 1) & (it < I + 1))
+        def _():
+            normed_gradient(it - 1)
+
     ng_recv[me] = ng_send[me]
+
+    @pl.loop(0, S)
+    def _(s):
+        @pl.when(s != me)
+        def _():
+            ng_copy(s, s).wait_recv()
+
+    tally = jnp.zeros((tok, 1), F32)
+    for j in range(I):
+        total = ng_recv[j * NT].astype(F32)
+        for h in range(1, NT):
+            total = total + ng_recv[j * NT + h].astype(F32)
+        for o in range(Z):
+            first = (o * I + j) * rows
+            term = gain_ref[:, first : first + rows] * total[:, o * rows : (o + 1) * rows]
+            terms[:, first : first + rows] = term
+            tally = tally + jnp.sum(unit_ref[:, first : first + rows] * term, axis=-1, keepdims=True)
+    mean = tally * (1.0 / (I * Z * rows))
+    grad_out[...] = (inverse_ref[...] * (terms[...] - unit_ref[...] * mean)).astype(BF16)
 
     @pl.loop(0, NC)
     def _(k):
@@ -335,19 +371,6 @@
     def _(s):
         @pl.when(s != me)
         def _():
-            ng_copy(s, s).wait_recv()
-
-    @pl.loop(0, I)
-    def _(j):
-        total = ng_recv[j * NT].astype(F32)
-        for h in range(1, NT):
-            total = total + ng_recv[j * NT + h].astype(F32)
-        grad_out[j] = total
-
-    @pl.loop(0, S)
-    def _(s):
-        @pl.when(s != me)
-        def _():
             normed_copy(s, me).wait_send()
             ng_copy(s, me).wait_send()
 
@@ -379,7 +402,7 @@
                 ag_left(k, d).wait_send()
 
 
-def fused(dims, factor, normed, gate_pre, up_pre, hidden_grad, gate_weight, up_weight):
+def fused(dims, factor, normed, gate_pre, up_pre, hidden_grad, gate_weight, up_weight, unit_rows, inverse, gain):
     Z, I, NT, NC, CW = dims
     X = I // CORES
     S = I * NT
@@ -392,11 +415,11 @@
     return pl.pallas_call(
         functools.partial(fused_kernel, dims, factor),
         out_shape=(
-            jax.ShapeDtypeStruct((I, tok, depth), F32),
+            jax.ShapeDtypeStruct((tok, I * depth), BF16),
             jax.ShapeDtypeStruct((rows, width), F32),
             jax.ShapeDtypeStruct((rows, width), F32),
         ),
-        in_specs=[vmem] * 6,
+        in_specs=[vmem] * 9,
         out_specs=(vmem, vmem, vmem),
         scratch_shapes=[
             pltpu.VMEM((NC, 2, I, slab, CW), BF16),
@@ -407,6 +430,7 @@
             pltpu.VMEM((slab, depth), F32),
             pltpu.VMEM((S, tok, depth), BF16),
             pltpu.VMEM((S, tok, depth), BF16),
+            pltpu.VMEM((tok, I * depth), F32),
             dma((NC, 2, Z)),
             dma((NC, Z)),
             dma((NC, Z)),
@@ -426,7 +450,7 @@
         cost_estimate=pl.CostEstimate(
             flops=8 * slab * I * depth * width, bytes_accessed=20 * 1024 * 1024, transcendentals=slab * width
         ),
-    )(normed, gate_pre, up_pre, hidden_grad, gate_weight, up_weight)
+    )(normed, gate_pre, up_pre, hidden_grad, gate_weight, up_weight, unit_rows, inverse, gain)
 
 
 def body(
@@ -454,15 +478,10 @@
     normed = (unit_rows * norm_gain).astype(BF16)
     blocks = normed.reshape(tok, Z, I, rows).transpose(2, 1, 3, 0).reshape(I, Z * rows, tok)
     factor = 1.0 / math.sqrt(gate_pre.shape[0] * count)
-    summed, gate_out, up_out = fused(
-        (Z, I, tensor, NC, CW), factor, blocks, gate_pre, up_pre, hidden_grad, gate_weight, up_weight
+    return fused(
+        (Z, I, tensor, NC, CW), factor, blocks, gate_pre, up_pre, hidden_grad, gate_weight, up_weight,
+        unit_rows, inverse, norm_gain[None, :],
     )
-    normed_grad = summed.reshape(I, tok, Z, rows).transpose(1, 2, 0, 3).reshape(tok, depth)
-    grad_term = norm_gain * normed_grad
-    input_grad = inverse * (
-        grad_term - unit_rows * jnp.mean(unit_rows * grad_term, axis=-1, keepdims=True)
-    )
-    return (input_grad.astype(BF16), gate_out, up_out)
 
 
 def solution(mesh):

time: 231 us -> 210 us (0.909)
  Pallas kernels: 215 us -> 197 us
    pallas_call x1, Pallas kernels: 215 us -> 197 us  [fused(): pl.pallas_call(functools.partial(fused_kernel, dims, factor), out_shape=(...]
    reshape x2 -> x0, local copies, waits for them, and re-layouts: 3.21 us -> none  [body(): summed.reshape(I, tok, Z, rows).transpose(1, 2, 0, 3).reshape(tok, depth)]
    unnamed x14 -> x9, local copies, waits for them, and re-layouts: 3.75 us -> 6.12 us
where the time goes in v2:
time: 210 us
  Pallas kernels  197 us (94%)
  local copies, waits for them, and re-layouts  8.47 us (4%)
  other arithmetic  3.96 us (2%)
    pallas_call x1, Pallas kernels, fused(): pl.pallas_call(functools.partial(fused_kernel, dims, factor), out_shape=(...  197 us
    unnamed x9, local copies, waits for them, and re-layouts  6.12 us

profile of v2, /device:TPU:0, one launch (start us, length us, event | category | flops | bytes accessed | tf_op | source)
XLA Modules:
  0.0 210.0 jit_solution(16172211414795017390)
XLA Ops:
  0.6 0.0 copy-start.1
  0.6 0.0 copy-start
  0.6 1.8 multiply_reduce_fusion
  2.5 0.8 copy.13.inverse_ref
  3.3 0.0 copy-done.1
  3.3 0.0 copy-done
  3.3 2.1 %multiply_convert_fusion = (bf16[128,2048]{1,0:T(8,128)(2,1)S(1)}, f32[128,2048]{1,0:T(8,128)}) fusion(f32[2048]{0:T(1024)} %param.12, f32[128]{0:T(128)S(1)} %get-tuple-element.6, f32[128]{0:T(128)} %param.11, s32[128,2048]{1,0:T(8,128)S(1)} %copy-done, bf16[128,2048]{1,0:T(8,128)(2,1)S(1)} %copy-done.1), kind=kLoop, calls=%fused_computation | loop fusion | flops 1835008 | bytes 3154944 | tf_op jit(solution)/shard_map/convert_element_type | solution.py:478
  5.4 0.4 reshape.35
  5.7 1.2 copy.12
  7.0 196.9 %shard_map.112 = (bf16[128,2048]{1,0:T(8,128)(2,1)}, f32[128,3584]{1,0:T(8,128)}, f32[128,3584]{1,0:T(8,128)}) custom-call(bf16[4,512,128]{2,1,0:T(8,128)(2,1)} %bitcast.6, bf16[256,3584]{1,0:T(8,128)(2,1)} %gate_ref.1, bf16[256,3584]{1,0:T(8,128)(2,1)} %up_ref.1, bf16[256,3584]{1,0:T(8,128)(2,1)} %hidden_ref.1, bf16[128,3584]{1,0:T(8,128)(2,1)} %gate_w_ref.1, ...), custom_call_target="tpu_custom_call" | custom-call | flops 15032385536 | bytes 20971520 | tf_op jit(solution)/shard_map/pallas_call | solution.py:415
  203.8 1.9 copy.17
  205.7 0.0 copy-start.2
  205.7 3.0 %copy.18 = f32[128,3584]{1,0:T(8,128)} copy(f32[128,3584]{1,0:T(8,128)} %get-tuple-element.11) | data formatting | bytes 3670016
  208.7 0.0 copy-done.2
  208.7 1.2 copy.19
  (1 shorter events, 0.0 us)
Async XLA Ops:
  0.6 2.6 %copy-start.1 = (bf16[128,2048]{1,0:T(8,128)(2,1)S(1)}, bf16[128,2048]{1,0:T(8,128)(2,1)}, u32[]{:S(2)}) copy-start(bf16[128,2048]{1,0:T(8,128)(2,1)} %param.10) | copy-start | bytes 1572868
  0.6 2.6 %copy-start = (s32[128,2048]{1,0:T(8,128)S(1)}, s32[128,2048]{1,0:T(8,128)}, u32[]{:S(2)}) copy-start(s32[128,2048]{1,0:T(8,128)} %param.9) | copy-start | bytes 3145732
  205.7 3.0 %copy-start.2 = (f32[128,3584]{1,0:T(8,128)S(1)}, f32[128,3584]{1,0:T(8,128)}, u32[]{:S(2)}) copy-start(f32[128,3584]{1,0:T(8,128)} %get-tuple-element.12) | copy-start | bytes 5505028

commit v3 on v2

--- a/solution.py
+++ b/solution.py
@@ -31,14 +31,14 @@
 def fused_kernel(
     dims,
     factor,
-    normed_ref,
+    quant_ref,
+    residual_ref,
+    scale_ref,
     gate_ref,
     up_ref,
     hidden_ref,
     gate_w_ref,
     up_w_ref,
-    unit_ref,
-    inverse_ref,
     gain_ref,
     grad_out,
     gate_out,
@@ -52,6 +52,9 @@
     ng_send,
     ng_recv,
     terms,
+    unit_ref,
+    inverse_ref,
+    normed_ref,
     ag_ss,
     ag_rs,
     rs_ss,
@@ -141,21 +144,31 @@
             normed_ref.at[lax.div(s, NT)], normed_all.at[:, place], n_ss.at[s], n_rs.at[source], member(s)
         )
 
+    @pl.loop(0, NC)
+    def _(k):
+        @pl.when(z < Z - 1)
+        def _():
+            ag_right(k, z).start()
+
+        @pl.when(z > 0)
+        def _():
+            ag_left(k, z).start()
+
+    summed_in = residual_ref[...].astype(F32) + quant_ref[...].astype(F32) * scale_ref[...]
+    inverse = lax.rsqrt(jnp.mean(summed_in * summed_in, axis=-1, keepdims=True) + 1e-05)
+    inverse_ref[...] = inverse
+    unit_ref[...] = summed_in * inverse
+    for j in range(I):
+        for o in range(Z):
+            first = (o * I + j) * rows
+            scaled_rows = unit_ref[:, first : first + rows] * gain_ref[:, first : first + rows]
+            normed_ref[j, o * rows : (o + 1) * rows] = scaled_rows.T.astype(BF16)
+
     @pl.loop(0, S)
     def _(s):
         @pl.when(s != me)
         def _():
             normed_copy(s, me).start()
-
-    @pl.loop(0, NC)
-    def _(k):
-        @pl.when(z < Z - 1)
-        def _():
-            ag_right(k, z).start()
-
-        @pl.when(z > 0)
-        def _():
-            ag_left(k, z).start()
 
     normed_all[:, pl.ds(pl.multiple_of(me * tok, 128), tok)] = normed_ref[i]
 
@@ -402,7 +415,7 @@
                 ag_left(k, d).wait_send()
 
 
-def fused(dims, factor, normed, gate_pre, up_pre, hidden_grad, gate_weight, up_weight, unit_rows, inverse, gain):
+def fused(dims, factor, quant_rows, residual, scale, gate_pre, up_pre, hidden_grad, gate_weight, up_weight, gain):
     Z, I, NT, NC, CW = dims
     X = I // CORES
     S = I * NT
@@ -431,6 +444,9 @@
             pltpu.VMEM((S, tok, depth), BF16),
             pltpu.VMEM((S, tok, depth), BF16),
             pltpu.VMEM((tok, I * depth), F32),
+            pltpu.VMEM((tok, I * depth), F32),
+            pltpu.VMEM((tok, 1), F32),
+            pltpu.VMEM((I, depth, tok), BF16),
             dma((NC, 2, Z)),
             dma((NC, Z)),
             dma((NC, Z)),
@@ -450,7 +466,7 @@
         cost_estimate=pl.CostEstimate(
             flops=8 * slab * I * depth * width, bytes_accessed=20 * 1024 * 1024, transcendentals=slab * width
         ),
-    )(normed, gate_pre, up_pre, hidden_grad, gate_weight, up_weight, unit_rows, inverse, gain)
+    )(quant_rows, residual, scale, gate_pre, up_pre, hidden_grad, gate_weight, up_weight, gain)
 
 
 def body(
@@ -468,19 +484,12 @@
     tensor = lax.axis_size("tensor")
     Z = line_length(count)
     I = count // Z
-    tok, depth = residual.shape
-    rows = gate_weight.shape[0]
     NC = chunk_count(gate_weight.shape[1])
     CW = gate_weight.shape[1] // NC
-    summed_in = residual.astype(F32) + quant_rows.astype(F32) * row_scale[:, None]
-    inverse = lax.rsqrt(jnp.mean(summed_in * summed_in, axis=-1, keepdims=True) + 1e-05)
-    unit_rows = summed_in * inverse
-    normed = (unit_rows * norm_gain).astype(BF16)
-    blocks = normed.reshape(tok, Z, I, rows).transpose(2, 1, 3, 0).reshape(I, Z * rows, tok)
     factor = 1.0 / math.sqrt(gate_pre.shape[0] * count)
     return fused(
-        (Z, I, tensor, NC, CW), factor, blocks, gate_pre, up_pre, hidden_grad, gate_weight, up_weight,
-        unit_rows, inverse, norm_gain[None, :],
+        (Z, I, tensor, NC, CW), factor, quant_rows, residual, row_scale[:, None],
+        gate_pre, up_pre, hidden_grad, gate_weight, up_weight, norm_gain[None, :],
     )
 
 

time: 210 us -> 206 us (0.981)
  other arithmetic: 3.96 us -> 0 us
    convert_element_type x1 -> x0, other arithmetic: 2.1 us -> none  [body(): normed = (unit_rows * norm_gain).astype(BF16)]
    unnamed x9 -> x5, local copies, waits for them, and re-layouts: 6.12 us -> 6.11 us
where the time goes in v3:
time: 206 us
  Pallas kernels  197 us (96%)
  local copies, waits for them, and re-layouts  7.5 us (4%)
    pallas_call x1, Pallas kernels, fused(): pl.pallas_call(functools.partial(fused_kernel, dims, factor), out_shape=(...  197 us
    unnamed x5, local copies, waits for them, and re-layouts  6.11 us

profile of v3, /device:TPU:0, one launch (start us, length us, event | category | flops | bytes accessed | tf_op | source)
XLA Modules:
  0.0 205.6 jit_solution(18381378284635735090)
XLA Ops:
  0.6 1.4 copy.12.scale_ref
  2.0 197.5 %shard_map.112 = (bf16[128,2048]{1,0:T(8,128)(2,1)}, f32[128,3584]{1,0:T(8,128)}, f32[128,3584]{1,0:T(8,128)}) custom-call(s32[128,2048]{1,0:T(8,128)} %quant_ref.1, bf16[128,2048]{1,0:T(8,128)(2,1)} %residual_ref.1, f32[128,1]{1,0:T(8,128)} %copy.12.scale_ref, bf16[256,3584]{1,0:T(8,128)(2,1)} %gate_ref.1, bf16[256,3584]{1,0:T(8,128)(2,1)} %up_ref.1, ...), custom_call_target="tpu_custom_call" | custom-call | flops 15032385536 | bytes 20971520 | tf_op jit(solution)/shard_map/pallas_call | solution.py:428
  199.5 1.9 copy.16
  201.4 0.0 copy-start
  201.4 3.0 %copy.17 = f32[128,3584]{1,0:T(8,128)} copy(f32[128,3584]{1,0:T(8,128)} %get-tuple-element.7) | data formatting | bytes 3670016
  204.4 0.0 copy-done
  204.4 1.2 copy.18
Async XLA Ops:
  201.4 3.0 %copy-start = (f32[128,3584]{1,0:T(8,128)S(1)}, f32[128,3584]{1,0:T(8,128)}, u32[]{:S(2)}) copy-start(f32[128,3584]{1,0:T(8,128)} %get-tuple-element.8) | copy-start | bytes 5505028
